TPU v7x, 128 devices: a whole 4x4x4 slice. The times are simulated.
128 devices in a mesh: row: 8 (over x_lo, z), col: 16 (over y, x_hi, core).
Axes of the slice: x: 4 (x_hi: 2, x_lo: 2; x = x_hi * 2 + x_lo), y: 4, z: 4, core: 2. Of those that a mesh axis runs over, the one named last changes fastest.
Arguments:
- examples: bfloat16 [262144, 1024], P(('row', 'col')), may hold values from -20 to 20
- residuals: float32 [262144, 256], P(('row', 'col')), may hold values from -6 to 6
- coefficients: float32 [262144, 256], P(('row', 'col')), may hold values from -0.8 to 0.8
- block_index: int32 [1], replicated, may hold values from 0 to 255
Outputs:
- new_residuals: float32 [262144, 256], P(('row', 'col'))
- new_coefficients: float32 [262144, 256], P(('row', 'col'))
All inputs are finite; a program needn't handle non-finite values.
Results may differ from a plain program's by a relative error of at most 0.00035.
Values may be sent and summed in bfloat16 or wider, within the bound.
A program may use at most 128 MiB of HBM per device.

v0:
```python
import jax
import jax.numpy as jnp
from jax import lax
from jax.sharding import PartitionSpec as P

BLOCK = 1024


ridge = 0.001
width_factor = 0.5


def spread(value, axis, source):
    kept = jnp.where(lax.axis_index(axis) == source, value, 0).astype(value.dtype)
    return lax.psum(kept, axis)


def body(examples, residuals, coefficients, block_index):
    rows_here = examples.shape[0]
    features = examples.shape[1]
    per_device = rows_here // BLOCK
    devices_all = lax.axis_size(("row", "col"))
    total_examples = rows_here * devices_all
    chosen = block_index[0]
    owner_rank = chosen // per_device
    offset = chosen % per_device * BLOCK
    my_rank = lax.axis_index(("row", "col"))
    is_owner = owner_rank == my_rank
    my_block = lax.dynamic_slice_in_dim(examples, offset, BLOCK, 0)
    block_rows = spread(my_block, ("row", "col"), owner_rank)
    sq_rows = jnp.sum(jnp.square(examples.astype(jnp.float32)), axis=1)
    sq_block = jnp.sum(jnp.square(block_rows.astype(jnp.float32)), axis=1)
    inner = lax.dot_general(
        examples, block_rows, (((1,), (1,)), ((), ())), preferred_element_type=jnp.float32
    )
    kernel = jnp.exp(
        -width_factor * (sq_rows[:, None] + sq_block[None, :] - 2.0 * inner) / features
    ).astype(jnp.bfloat16)
    residual_low = residuals.astype(jnp.bfloat16)
    grad_part = lax.dot_general(
        kernel, residual_low, (((0,), (0,)), ((), ())), preferred_element_type=jnp.float32
    )
    gram_part = lax.dot_general(
        kernel, kernel, (((0,), (0,)), ((), ())), preferred_element_type=jnp.float32
    )
    own_coef = lax.dynamic_slice_in_dim(coefficients, offset, BLOCK, 0)
    weight_own = jnp.where(is_owner, total_examples * ridge, 0.0).astype(jnp.float32)
    grad_part = grad_part - weight_own * own_coef
    grad, gram_sum = lax.psum((grad_part, gram_part), ("row", "col"))
    system = gram_sum / total_examples + ridge * jnp.eye(BLOCK, dtype=jnp.float32)
    factor = jnp.linalg.cholesky(system)
    update = jax.scipy.linalg.cho_solve((factor, True), grad / total_examples)
    update_low = update.astype(jnp.bfloat16)
    new_residuals = residuals - jnp.dot(kernel, update_low, preferred_element_type=jnp.float32)
    updated = lax.dynamic_update_slice_in_dim(coefficients, own_coef + update, offset, 0)
    new_coefficients = jnp.where(is_owner, updated, coefficients)
    return (new_residuals, new_coefficients)


def solution(mesh):
    in_specs = (P(("row", "col"), None), P(("row", "col"), None), P(("row", "col"), None), P())
    out_specs = (P(("row", "col"), None), P(("row", "col"), None))
    return jax.shard_map(body, mesh=mesh, in_specs=in_specs, out_specs=out_specs, check_vma=False)
```

profile of v0, /device:TPU:1, one launch (start us, length us, event | category | flops | bytes accessed | tf_op | source)
XLA Modules:
  0.0 713.0 jit_solution(15090912758138508749)
XLA Ops:
  7.2 1.6 copy.99
  9.5 3.4 dynamic-slice_select_fusion
  13.0 3.1 multiply_reduce_fusion
  16.1 150.9 %all-reduce.5.cloned.1.call-done = bf16[1024,1024]{1,0:T(8,128)(2,1)} async-done(((bf16[1024,1024]{1,0:T(8,128)(2,1)}), bf16[1024,1024]{1,0:T(8,128)(2,1)}) %all-reduce.5.cloned.1.call-update) | async-done | bytes 2097168 | tf_op jit(solution)/shard_map/psum | solution.py:15
  167.0 2.1 multiply_reduce_fusion.1
  169.1 7.9 %fusion.2 = bf16[2048,1024]{0,1:T(8,128)(2,1)S(1)} fusion(bf16[1024,1024]{1,0:T(8,128)(2,1)} %all-reduce.5.cloned.1.call-done, bf16[2048,1024]{1,0:T(8,128)(2,1)} %param.4, f32[1024]{0:T(1024)S(1)} %multiply_reduce_fusion.1, f32[2048]{0:T(1024)S(1)} %multiply_reduce_fusion), kind=kOutput, calls=%fused_computation.5 | convolution fusion | flops 4305453056 | bytes 10498048 | tf_op jit(solution)/shard_map/dot_general | solution.py:33
  177.0 6.1 fusion.101
  183.0 2.2 convolution_subtract_fusion.1
  185.3 154.7 %all-reduce.7.cloned.1.call-done = (f32[1024,256]{1,0:T(8,128)}, f32[1024,1024]{0,1:T(8,128)}) async-done(((f32[1024,256]{1,0:T(8,128)}, f32[1024,1024]{0,1:T(8,128)}), (f32[1024,256]{1,0:T(8,128)}, f32[1024,1024]{0,1:T(8,128)})) %all-reduce.7.cloned.1.call-update) | async-done | bytes 5242896 | tf_op jit(solution)/shard_map/psum | solution.py:49
  340.0 5.0 select_add_fusion
  345.0 5.5 copy.7
  350.5 4.5 fusion.3
  355.0 2.0 copy-done.1
  356.9 11.7 %cholesky.222 = f32[128,128]{1,0:T(8,128)S(1)} custom-call(f32[128,128]{1,0:T(8,128)S(1)} %cholesky.577), custom_call_target="Cholesky" | custom-call | tf_op jit(solution)/shard_map/jit(cholesky)/cholesky | solution.py:51
  368.8 9.8 %custom-call.66 = f32[1,128,128]{1,2,0:T(8,128)S(1)} custom-call(f32[1,128,128]{2,1,0:T(8,128)S(1)} %get-tuple-element.56), custom_call_target="InvertDiagBlocksLowerTriangular" | custom-call | tf_op jit(solution)/shard_map/jit(cholesky)/cholesky | solution.py:51
  378.6 1.5 fusion.29
  380.4 1.6 convolution_subtract_fusion.2
  382.7 11.7 %cholesky.243 = f32[128,128]{1,0:T(8,128)S(1)} custom-call(f32[128,128]{1,0:T(8,128)S(1)} %cholesky.581), custom_call_target="Cholesky" | custom-call | tf_op jit(solution)/shard_map/jit(cholesky)/cholesky | solution.py:51
  394.7 2.5 cholesky.254
  397.3 9.8 %custom-call.67 = f32[1,128,128]{1,2,0:T(8,128)S(1)} custom-call(f32[1,128,128]{2,1,0:T(8,128)S(1)} %get-tuple-element.54), custom_call_target="InvertDiagBlocksLowerTriangular" | custom-call | tf_op jit(solution)/shard_map/jit(cholesky)/cholesky | solution.py:51
  408.6 1.3 convolution_dynamic-update-slice_fusion
  409.9 2.7 convolution_subtract_fusion.3
  412.6 11.7 %cholesky.466 = f32[128,128]{1,0:T(8,128)S(1)} custom-call(f32[128,128]{1,0:T(8,128)S(1)} %cholesky.586), custom_call_target="Cholesky" | custom-call | tf_op jit(solution)/shard_map/jit(cholesky)/cholesky | solution.py:51
  425.1 9.8 %custom-call.68 = f32[1,128,128]{1,2,0:T(8,128)S(1)} custom-call(f32[1,128,128]{2,1,0:T(8,128)S(1)} %get-tuple-element.52), custom_call_target="InvertDiagBlocksLowerTriangular" | custom-call | tf_op jit(solution)/shard_map/jit(cholesky)/cholesky | solution.py:51
  434.9 1.2 convolution_dynamic-update-slice_fusion.1
  436.1 3.5 convolution_subtract_fusion.4
  439.7 11.7 %cholesky.485 = f32[128,128]{1,0:T(8,128)S(1)} custom-call(f32[128,128]{1,0:T(8,128)S(1)} %cholesky.591), custom_call_target="Cholesky" | custom-call | tf_op jit(solution)/shard_map/jit(cholesky)/cholesky | solution.py:51
  452.2 9.8 %custom-call.69 = f32[1,128,128]{1,2,0:T(8,128)S(1)} custom-call(f32[1,128,128]{2,1,0:T(8,128)S(1)} %get-tuple-element.50), custom_call_target="InvertDiagBlocksLowerTriangular" | custom-call | tf_op jit(solution)/shard_map/jit(cholesky)/cholesky | solution.py:51
  462.0 1.1 convolution_dynamic-update-slice_fusion.2
  463.1 3.2 convolution_subtract_fusion.5
  466.3 11.9 %cholesky.504 = f32[128,128]{1,0:T(8,128)S(1)} custom-call(f32[128,128]{1,0:T(8,128)S(1)} %cholesky.596), custom_call_target="Cholesky" | custom-call | tf_op jit(solution)/shard_map/jit(cholesky)/cholesky | solution.py:51
  478.9 9.8 %custom-call.70 = f32[1,128,128]{1,2,0:T(8,128)S(1)} custom-call(f32[1,128,128]{2,1,0:T(8,128)S(1)} %get-tuple-element.48), custom_call_target="InvertDiagBlocksLowerTriangular" | custom-call | tf_op jit(solution)/shard_map/jit(cholesky)/cholesky | solution.py:51
  488.8 1.1 convolution_dynamic-update-slice_fusion.3
  489.9 3.2 convolution_subtract_fusion.6
  493.1 11.7 %cholesky.524 = f32[128,128]{1,0:T(8,128)S(1)} custom-call(f32[128,128]{1,0:T(8,128)S(1)} %cholesky.601), custom_call_target="Cholesky" | custom-call | tf_op jit(solution)/shard_map/jit(cholesky)/cholesky | solution.py:51
  505.6 9.8 %custom-call.71 = f32[1,128,128]{1,2,0:T(8,128)S(1)} custom-call(f32[1,128,128]{2,1,0:T(8,128)S(1)} %get-tuple-element.46), custom_call_target="InvertDiagBlocksLowerTriangular" | custom-call | tf_op jit(solution)/shard_map/jit(cholesky)/cholesky | solution.py:51
  515.4 1.0 convolution_dynamic-update-slice_fusion.5
  516.4 3.1 convolution_subtract_fusion.19
  519.6 11.7 %cholesky.544 = f32[128,128]{1,0:T(8,128)S(1)} custom-call(f32[128,128]{1,0:T(8,128)S(1)} %cholesky.606), custom_call_target="Cholesky" | custom-call | tf_op jit(solution)/shard_map/jit(cholesky)/cholesky | solution.py:51
  532.1 9.8 %custom-call.72 = f32[1,128,128]{1,2,0:T(8,128)S(1)} custom-call(f32[1,128,128]{2,1,0:T(8,128)S(1)} %get-tuple-element.44), custom_call_target="InvertDiagBlocksLowerTriangular" | custom-call | tf_op jit(solution)/shard_map/jit(cholesky)/cholesky | solution.py:51
  542.8 2.2 convolution_subtract_fusion.22
  545.0 11.7 %cholesky.562 = f32[128,128]{1,0:T(8,128)S(1)} custom-call(f32[128,128]{1,0:T(8,128)S(1)} %convolution_subtract_fusion.22), custom_call_target="Cholesky" | custom-call | tf_op jit(solution)/shard_map/jit(cholesky)/cholesky | solution.py:51
  556.9 1.3 broadcast_multiply_fusion
  568.4 4.9 select_select_fusion
  573.3 28.3 %while.1 = (s32[]{:T(128)}, f32[1024,1024]{0,1:T(8,128)}, s32[8,2]{0,1:T(2,128)S(1)}, f32[8,128,128]{2,1,0:T(8,128)}, s32[]{:T(128)}) while((s32[]{:T(128)}, f32[1024,1024]{0,1:T(8,128)}, s32[8,2]{0,1:T(2,128)S(1)}, f32[8,128,128]{2,1,0:T(8,128)}, s32[]{:T(128)}) %tuple.53), condition=%wide.while_cond, body=%wide.while_body.sunk | while | flops 2 | bytes 393329 | solution.py:52
  573.9 2.2 dynamic-slice.9
  577.4 2.2 dynamic-slice.9
  581.0 2.2 dynamic-slice.9
  584.5 2.2 dynamic-slice.9
  588.1 2.2 dynamic-slice.9
  591.6 2.2 dynamic-slice.9
  595.2 2.2 dynamic-slice.9
  598.7 2.1 dynamic-slice.9
  601.6 80.2 %custom-call.73 = f32[8,128,128]{1,2,0:T(8,128)} custom-call(f32[8,128,128]{2,1,0:T(8,128)} %get-tuple-element.9), custom_call_target="InvertDiagBlocksLowerTriangular" | custom-call | tf_op jit(solution)/shard_map/jit(_cho_solve)/triangular_solve | solution.py:52
  681.8 1.3 constant_dynamic-update-slice_fusion.10
  683.1 1.3 convolution_subtract_fusion.18
  684.4 1.2 constant_dynamic-update-slice_fusion.9
  685.6 1.3 convolution_subtract_fusion.14
  686.9 1.2 constant_dynamic-update-slice_fusion.8
  688.1 1.4 convolution_subtract_fusion.13
  689.5 1.2 constant_dynamic-update-slice_fusion.7
  693.9 1.0 convolution_subtract_fusion.21
  701.6 2.8 convolution_subtract_fusion
  704.7 1.3 copy-done.4
  (142 shorter events, 33.8 us)
Async XLA Ops:
  7.2 159.8 %all-reduce.5.cloned.1.call-start = ((), (), s32[]{:S(2)}) async-start(), calls=%async_computation | async-start | bytes 4194304 | tf_op jit(solution)/shard_map/psum | solution.py:15
  13.0 327.0 %all-reduce.7.cloned.1.call-start = ((), (), s32[]{:S(2)}) async-start(), calls=%async_computation.1 | async-start | bytes 10485760 | tf_op jit(solution)/shard_map/psum | solution.py:49
  176.9 6.1 copy-start.2
  176.9 6.1 copy-start.5
  355.0 2.0 copy-start.1
  381.9 0.8 copy-start.8
  382.7 25.9 %copy-start.9 = (f32[896,128]{1,0:T(8,128)S(1)}, f32[896,128]{1,0:T(8,128)}, u32[]{:S(2)}) copy-start(f32[896,128]{1,0:T(8,128)} %copy-done.8) | copy-start | bytes 1376260
  681.8 8.8 %copy-start = (f32[1024,1024]{0,1:T(8,128)S(1)}, f32[1024,1024]{0,1:T(8,128)}, u32[]{:S(2)}) copy-start(f32[1024,1024]{0,1:T(8,128)} %get-tuple-element.124) | copy-start | bytes 12582916
  681.8 9.5 %copy-start.7 = (f32[8,128,128]{1,2,0:T(8,128)S(1)}, f32[8,128,128]{1,2,0:T(8,128)}, u32[]{:S(2)}) copy-start(f32[8,128,128]{1,2,0:T(8,128)} %custom-call.73) | copy-start | bytes 1572868
  698.8 2.2 copy-start.3
  698.8 2.9 copy-start.6
  704.6 1.3 copy-start.4
Sparse Core Ops, SparseCore 0:
  13.4 153.5 all-reduce.4
  185.4 154.5 all-reduce.6
where the time goes:
time: 722 us; the launch traced here: 713 us
  waiting for transfers between devices  306 us (42%)
  other arithmetic  272 us (38%)
  matrix products  65 us (9%)
  local copies, waits for them, and re-layouts  49.5 us (7%)
  between operations  20.7 us (3%)
    another operation x30, other arithmetic, body(): factor = jnp.linalg.cholesky(system)  167 us
    psum x1, waiting for transfers between devices, body(): grad, gram_sum = lax.psum((grad_part, gram_part), ('row', 'col'))  155 us
    psum x1, waiting for transfers between devices, spread(): return lax.psum(kept, axis)  151 us
    another operation x3, other arithmetic, body(): update = jax.scipy.linalg.cho_solve((factor, True), grad / total_examples)  85.1 us
    another operation x40, local copies, waits for them, and re-layouts  28.2 us
    another operation x14, matrix products, body(): factor = jnp.linalg.cholesky(system)  27.7 us
    another operation x30, matrix products, body(): update = jax.scipy.linalg.cho_solve((factor, True), grad / total_examples)  18.3 us
  transfers between devices with their start and end apart: 2, of which 2 were waited for; matrix products, arithmetic and copies ran while one was open for 0% of the time, Pallas kernels for 0%

commit v1 on v0

--- a/solution.py
+++ b/solution.py
@@ -1,6 +1,9 @@
+import functools
 import jax
 import jax.numpy as jnp
 from jax import lax
+from jax.experimental import pallas as pl
+from jax.experimental.pallas import tpu as pltpu
 from jax.sharding import PartitionSpec as P
 
 BLOCK = 1024
@@ -8,6 +11,99 @@
 
 ridge = 0.001
 width_factor = 0.5
+
+HI = lax.Precision.HIGHEST
+NB = 128
+
+def dot(a, b, ca, cb):
+    return lax.dot_general(a, b, (((ca,), (cb,)), ((), ())), precision=HI, preferred_element_type=jnp.float32)
+
+def split3(v):
+    h = v.astype(jnp.bfloat16).astype(jnp.float32)
+    r = v - h
+    m = r.astype(jnp.bfloat16).astype(jnp.float32)
+    return h, m, r - m
+
+def factor(M):
+    sub = lax.broadcasted_iota(jnp.int32, (8, 128), 0)
+    sub2 = lax.broadcasted_iota(jnp.int32, (8, 256), 0)
+    lane = lax.broadcasted_iota(jnp.int32, (8, 128), 1)
+    for q in range(16):
+        r0 = 8 * q
+        look = q < 15
+        top = M[r0:r0 + 8, :]
+        ct = [jnp.broadcast_to(top[:, r0 + j:r0 + j + 1], (8, 128)) for j in range(8)]
+        if look:
+            bot = M[r0 + 8:r0 + 16, :]
+            cb = [jnp.broadcast_to(bot[:, r0 + j:r0 + j + 1], (8, 128)) for j in range(8)]
+        for j in range(8):
+            r = lax.rsqrt(ct[j][j:j + 1, :])
+            r2 = jnp.concatenate([r, r], axis=1)
+            row = top[j:j + 1, :] * r2
+            mt = jnp.where(sub > j, ct[j] * r, 0.0)
+            mt2 = jnp.concatenate([mt, mt], axis=1)
+            rows_k = {k: ct[k][j:j + 1, :] * r for k in range(j + 1, 8)}
+            top = jnp.where(sub2 == j, row, top - mt2 * row)
+            for k in range(j + 1, 8):
+                ct[k] = ct[k] - mt * rows_k[k]
+            if look:
+                mb = cb[j] * r
+                mb2 = jnp.concatenate([mb, mb], axis=1)
+                bot = bot - mb2 * row
+                for k in range(j + 1, 8):
+                    cb[k] = cb[k] - mb * rows_k[k]
+        M[r0:r0 + 8, :] = top
+        if look:
+            M[r0 + 8:r0 + 16, :] = bot
+        if q < 14:
+            h, m, l = split3(top)
+            keep = lane >= r0 + 16
+            hl, ml, ll = [jnp.where(keep, v[:, :128], 0.0) for v in (h, m, l)]
+            lhs = jnp.concatenate([hl, hl, ml, hl, ml, ll], axis=0).astype(jnp.bfloat16)
+            rhs = jnp.concatenate([h, m, h, l, m, h], axis=0).astype(jnp.bfloat16)
+            res = lax.dot_general(lhs, rhs, (((0,), (0,)), ((), ())), preferred_element_type=jnp.float32)
+            M[r0 + 16:, :] = M[r0 + 16:, :] - res[r0 + 16:, :]
+
+def solve_kernel(scale, ridge, gram_ref, grad_ref, upd_ref, low_ref, S, G, M, W):
+    n = gram_ref.shape[0]
+    nb = n // NB
+    eye = (lax.broadcasted_iota(jnp.int32, (NB, NB), 0) == lax.broadcasted_iota(jnp.int32, (NB, NB), 1)).astype(jnp.float32)
+    S[...] = gram_ref[...] * scale
+    G[...] = grad_ref[...] * scale
+    for k in range(nb):
+        a, b = k * NB, (k + 1) * NB
+        M[:, :NB] = S[a:b, a:b] + ridge * eye
+        M[:, NB:] = eye
+        factor(M)
+        w = M[:, NB:]
+        W[a:b, :] = w
+        G[a:b, :] = dot(w, G[a:b, :], 1, 0)
+        if k < nb - 1:
+            u = dot(w, S[a:b, b:], 1, 0)
+            l = dot(S[b:, a:b], w, 1, 1)
+            S[a:b, b:] = u
+            S[b:, b:] = S[b:, b:] - dot(l, u, 1, 0)
+            G[b:, :] = G[b:, :] - dot(l, G[a:b, :], 1, 0)
+    for k in reversed(range(nb)):
+        a, b = k * NB, (k + 1) * NB
+        y = G[a:b, :]
+        if k < nb - 1:
+            y = y - dot(S[a:b, b:], G[b:, :], 1, 0)
+        G[a:b, :] = dot(W[a:b, :], y, 0, 0)
+    upd_ref[...] = G[...]
+    low_ref[...] = G[...].astype(jnp.bfloat16)
+
+def solve(gram, grad, total, ridge):
+    n, o = grad.shape
+    return pl.pallas_call(
+        functools.partial(solve_kernel, 1.0 / total, ridge),
+        out_shape=(jax.ShapeDtypeStruct((n, o), jnp.float32), jax.ShapeDtypeStruct((n, o), jnp.bfloat16)),
+        in_specs=[pl.BlockSpec(memory_space=pltpu.VMEM)] * 2,
+        out_specs=[pl.BlockSpec(memory_space=pltpu.VMEM)] * 2,
+        scratch_shapes=[pltpu.VMEM((n, n), jnp.float32), pltpu.VMEM((n, o), jnp.float32), pltpu.VMEM((NB, 2 * NB), jnp.float32), pltpu.VMEM((n, NB), jnp.float32)],
+        compiler_params=pltpu.CompilerParams(vmem_limit_bytes=48 * 2**20),
+        name="solve_block",
+    )(gram, grad)
 
 
 def spread(value, axis, source):
@@ -47,10 +143,7 @@
     weight_own = jnp.where(is_owner, total_examples * ridge, 0.0).astype(jnp.float32)
     grad_part = grad_part - weight_own * own_coef
     grad, gram_sum = lax.psum((grad_part, gram_part), ("row", "col"))
-    system = gram_sum / total_examples + ridge * jnp.eye(BLOCK, dtype=jnp.float32)
-    factor = jnp.linalg.cholesky(system)
-    update = jax.scipy.linalg.cho_solve((factor, True), grad / total_examples)
-    update_low = update.astype(jnp.bfloat16)
+    update, update_low = solve(gram_sum, grad, total_examples, ridge)
     new_residuals = residuals - jnp.dot(kernel, update_low, preferred_element_type=jnp.float32)
     updated = lax.dynamic_update_slice_in_dim(coefficients, own_coef + update, offset, 0)
     new_coefficients = jnp.where(is_owner, updated, coefficients)

time: 722 us -> 411 us (0.57)
  other arithmetic: 272 us -> 8.78 us
  Pallas kernels: 0 us -> 52.2 us
  local copies, waits for them, and re-layouts: 49.5 us -> 2.84 us
  matrix products: 65 us -> 19.4 us
    another operation x33 -> x0, other arithmetic: 252 us -> none  [the longest x30 167 us: body(): factor = jnp.linalg.cholesky(system)]
    pallas_call x0 -> x1, Pallas kernels: none -> 52.2 us  [solve(): pl.pallas_call(functools.partial(solve_kernel, 1.0 / total, ridge), out_s...]
    another operation x44 -> x0, matrix products: 46 us -> none  [the longest x14 27.7 us: body(): factor = jnp.linalg.cholesky(system)]
    another operation x70 -> x0, local copies, waits for them, and re-layouts: 37.4 us -> none
  transfers between devices with their start and end apart: 2 -> 2, of which waited for: 2 -> 2; matrix products, arithmetic and copies ran while one was open for 0% -> 1% of each run, Pallas kernels for 0% -> 0%
where the time goes in v1:
time: 411 us; the launch traced here: 404 us
  waiting for transfers between devices  306 us (74%)
  Pallas kernels  52.2 us (13%)
  matrix products  19.4 us (5%)
  between operations  15.1 us (4%)
  other arithmetic  8.78 us (2%)
    psum x1, waiting for transfers between devices, body(): grad, gram_sum = lax.psum((grad_part, gram_part), ('row', 'col'))  155 us
    psum x1, waiting for transfers between devices, spread(): return lax.psum(kept, axis)  151 us
    pallas_call x1, Pallas kernels, solve(): pl.pallas_call(functools.partial(solve_kernel, 1.0 / total, ridge), out_s...  52.2 us
  transfers between devices with their start and end apart: 2, of which 2 were waited for; matrix products, arithmetic and copies ran while one was open for 1% of the time, Pallas kernels for 0%

profile of v1, /device:TPU:1, one launch (start us, length us, event | category | flops | bytes accessed | tf_op | source)
XLA Modules:
  0.0 404.3 jit_solution(18083511705549276185)
XLA Ops:
  7.2 0.0 all-reduce.4.cloned.1.call-start
  7.2 1.6 copy.12
  9.5 3.4 dynamic-slice_select_fusion
  12.9 0.0 all-reduce.4.cloned.1.call-update
  13.0 0.0 all-reduce.6.cloned.1.call-start
  13.0 3.1 multiply_reduce_fusion
  16.1 150.9 %all-reduce.4.cloned.1.call-done = bf16[1024,1024]{1,0:T(8,128)(2,1)} async-done(((bf16[1024,1024]{1,0:T(8,128)(2,1)}), bf16[1024,1024]{1,0:T(8,128)(2,1)}) %all-reduce.4.cloned.1.call-update) | async-done | bytes 2097168 | tf_op jit(solution)/shard_map/psum | solution.py:111
  167.0 2.1 multiply_reduce_fusion.1
  169.1 7.9 %fusion.2 = bf16[2048,1024]{0,1:T(8,128)(2,1)S(1)} fusion(bf16[1024,1024]{1,0:T(8,128)(2,1)} %all-reduce.4.cloned.1.call-done, bf16[2048,1024]{1,0:T(8,128)(2,1)} %param.4, f32[1024]{0:T(1024)S(1)} %multiply_reduce_fusion.1, f32[2048]{0:T(1024)S(1)} %multiply_reduce_fusion), kind=kOutput, calls=%fused_computation.3 | convolution fusion | flops 4305453056 | bytes 10498048 | tf_op jit(solution)/shard_map/dot_general | solution.py:129
  177.0 0.0 copy-start.4
  177.0 0.0 copy-start.2
  177.0 6.6 %fusion.5 = f32[1024,1024]{1,0:T(8,128)} fusion(bf16[2048,1024]{0,1:T(8,128)(2,1)S(1)} %fusion.2), kind=kOutput, calls=%fused_computation.12 | convolution fusion | flops 4294967296 | bytes 8388608 | tf_op jit(solution)/shard_map/dot_general | solution.py:139
  183.6 0.0 copy-done.4
  183.6 0.0 copy-done.2
  183.6 2.3 convolution_subtract_fusion.1
  185.9 0.0 all-reduce.6.cloned.1.call-update
  185.9 154.9 %all-reduce.6.cloned.1.call-done = (f32[1024,1024]{1,0:T(8,128)}, f32[1024,256]{1,0:T(8,128)}) async-done(((f32[1024,1024]{1,0:T(8,128)}, f32[1024,256]{1,0:T(8,128)}), (f32[1024,1024]{1,0:T(8,128)}, f32[1024,256]{1,0:T(8,128)})) %all-reduce.6.cloned.1.call-update) | async-done | bytes 5242896 | tf_op jit(solution)/shard_map/psum | solution.py:145
  340.8 0.0 copy-start
  340.8 1.2 copy-done
  342.0 0.0 copy-start.3
  342.1 0.0 copy-start.5
  342.1 52.2 %solve_block.1 = (f32[1024,256]{1,0:T(8,128)S(1)}, bf16[1024,256]{1,0:T(8,128)(2,1)S(1)}) custom-call(f32[1024,1024]{1,0:T(8,128)} %get-tuple-element.6.gram_ref, f32[1024,256]{1,0:T(8,128)S(1)} %copy-done), custom_call_target="tpu_custom_call" | custom-call | tf_op jit(solution)/shard_map/solve_block/pallas_call | solution.py:98
  394.3 0.2 fusion.3
  394.5 0.0 copy-start.1
  394.5 0.0 copy-done.3
  394.5 0.0 copy-done.5
  394.5 2.7 convolution_subtract_fusion
  397.2 0.0 copy-done.1
Async XLA Ops:
  7.2 159.9 %all-reduce.4.cloned.1.call-start = ((), (), s32[]{:S(2)}) async-start(), calls=%async_computation | async-start | bytes 4194304 | tf_op jit(solution)/shard_map/psum | solution.py:111
  13.0 327.9 %all-reduce.6.cloned.1.call-start = ((), (), s32[]{:S(2)}) async-start(), calls=%async_computation.1 | async-start | bytes 10485760 | tf_op jit(solution)/shard_map/psum | solution.py:145
  177.0 6.6 %copy-start.4 = (bf16[2048,1024]{0,1:T(8,128)(2,1)}, bf16[2048,1024]{0,1:T(8,128)(2,1)S(1)}, u32[]{:S(2)}) copy-start(bf16[2048,1024]{0,1:T(8,128)(2,1)S(1)} %fusion.2) | copy-start | bytes 12582916
  177.0 6.6 %copy-start.2 = (f32[2048,256]{1,0:T(8,128)S(1)}, f32[2048,256]{1,0:T(8,128)}, u32[]{:S(2)}) copy-start(f32[2048,256]{1,0:T(8,128)} %param.5) | copy-start | bytes 6291460
  340.8 1.2 copy-start
  342.0 52.5 %copy-start.3 = (f32[2048,256]{1,0:T(8,128)S(1)}, f32[2048,256]{1,0:T(8,128)}, u32[]{:S(2)}) copy-start(f32[2048,256]{1,0:T(8,128)} %param.5) | copy-start | bytes 6291460
  342.1 52.5 %copy-start.5 = (bf16[2048,1024]{0,1:T(8,128)(2,1)S(1)}, bf16[2048,1024]{0,1:T(8,128)(2,1)}, u32[]{:S(2)}) copy-start(bf16[2048,1024]{0,1:T(8,128)(2,1)} %copy-done.4) | copy-start | bytes 12582916
  394.5 2.7 copy-start.1
Sparse Core Ops, SparseCore 0:
  13.4 153.5 all-reduce.3
  186.0 154.7 all-reduce.5
